TPU v7x, 32 devices: a whole 2x2x4 slice. The times are simulated.
32 devices in a mesh: band: 2 (over y), stn: 4 (over z), tm: 4 (over x, core).
Axes of the slice: x: 2, y: 2, z: 4, core: 2. Of those that a mesh axis runs over, the one named last changes fastest.
Arguments:
- samples: bfloat16 [8, 524288], P(('band', 'stn'), 'tm'), parts along dimension 0, may hold values from -6 to 6
- delays: int32 [4, 4], P('stn', 'tm'), may hold values from 0 to 24576, as said below
- fringe: int32 [8, 64], P(('band', 'stn'), 'tm'), parts along dimension 0, may hold values from 0 to 65535
Outputs:
- visibility: float32 [2, 8, 4, 4096], P(None, ('band', 'stn'), None, 'tm'), parts along dimension 1
There are 2 independent parts, one for each index of `band`. A program takes and returns all parts, laid end to end along the dimension named above; an argument that names none is the same for every part. Nothing has to cross between parts.
Inputs may be any that keep to these rules, and one draw needn't show every extreme that they name: delays lie in 0 to 24576; 24576 is reached in every draw.
All inputs are finite; a program needn't handle non-finite values.
Results may differ from a plain program's by a relative error of at most 0.0017.
Values may be sent and summed in bfloat16 or wider, within the bound.
A program may use at most 64 MiB of HBM per device.

v0:
```python
import jax
import jax.numpy as jnp
from jax import lax
from jax.sharding import PartitionSpec as P

SPAN = 8192
DMAX = 24576


def shifted(block, axis, distance):
    devices = range(lax.axis_size(axis))
    route = [(i - distance, i) for i in devices if i - distance in devices]
    return lax.ppermute(block, axis, route)


def passed_along(value, axis, by):
    size = lax.axis_size(axis)
    return lax.ppermute(value, axis, [(i, (i + by) % size) for i in range(size)])


def dft_tables():
    first_index = jnp.arange(64, dtype=jnp.int32)
    second_index = jnp.arange(128, dtype=jnp.int32)
    first_phase = (
        2.0 * jnp.pi * (first_index[:, None] * first_index[None, :] % 64).astype(jnp.float32) / 64.0
    )
    twist_phase = (
        2.0
        * jnp.pi
        * (first_index[:, None] * second_index[None, :] % 8192).astype(jnp.float32)
        / 8192.0
    )
    second_phase = (
        2.0
        * jnp.pi
        * (second_index[:, None] * first_index[None, :] % 128).astype(jnp.float32)
        / 128.0
    )
    return (first_phase, twist_phase, second_phase)


def spectrum(aligned, turn_table):
    stations, frames, span = aligned.shape
    first_phase, twist_phase, second_phase = dft_tables()
    high = lax.Precision.HIGHEST
    signal = aligned.astype(jnp.float32).reshape(stations, frames, 64, 128)
    first_real = jnp.einsum("sfab,ak->sfkb", signal, jnp.cos(first_phase), precision=high)
    first_imag = -jnp.einsum("sfab,ak->sfkb", signal, jnp.sin(first_phase), precision=high)
    cos_twist = jnp.cos(twist_phase)
    sin_twist = jnp.sin(twist_phase)
    twist_real = first_real * cos_twist + first_imag * sin_twist
    twist_imag = first_imag * cos_twist - first_real * sin_twist
    cos_second = jnp.cos(second_phase)
    sin_second = jnp.sin(second_phase)
    out_real = jnp.einsum("sfkb,bq->sfqk", twist_real, cos_second, precision=high) + jnp.einsum(
        "sfkb,bq->sfqk", twist_imag, sin_second, precision=high
    )
    out_imag = jnp.einsum("sfkb,bq->sfqk", twist_imag, cos_second, precision=high) - jnp.einsum(
        "sfkb,bq->sfqk", twist_real, sin_second, precision=high
    )
    norm_factor = 1.0 / jnp.sqrt(jnp.float32(span))
    out_real = out_real.reshape(stations, frames, span // 2) * norm_factor
    out_imag = out_imag.reshape(stations, frames, span // 2) * norm_factor
    phase_angle = (2.0 * jnp.pi * turn_table.astype(jnp.float32) / 65536.0)[:, :, None]
    cos_fringe = jnp.cos(phase_angle)
    sin_fringe = jnp.sin(phase_angle)
    rotated_real = out_real * cos_fringe + out_imag * sin_fringe
    rotated_imag = out_imag * cos_fringe - out_real * sin_fringe
    return jnp.stack([rotated_real, rotated_imag]).astype(jnp.bfloat16)


def cross(left_spec, right_spec):
    f32 = jnp.float32
    real_part = jnp.einsum(
        "afk,bfk->abk", left_spec[0], right_spec[0], preferred_element_type=f32
    ) + jnp.einsum("afk,bfk->abk", left_spec[1], right_spec[1], preferred_element_type=f32)
    imag_part = jnp.einsum(
        "afk,bfk->abk", left_spec[1], right_spec[0], preferred_element_type=f32
    ) - jnp.einsum("afk,bfk->abk", left_spec[0], right_spec[1], preferred_element_type=f32)
    return jnp.stack([real_part, imag_part])


def place(current_totals, block_term, first_station):
    current = lax.dynamic_slice_in_dim(current_totals, first_station, block_term.shape[2], 2)
    return lax.dynamic_update_slice_in_dim(current_totals, current + block_term, first_station, 2)


def on_device(samples, delays, fringe):
    stn_here, length = samples.shape
    frames_here = length // SPAN
    next_head = shifted(samples[:, :DMAX], "tm", -1)
    joined = jnp.concatenate([samples, next_head], axis=1)

    def take(sample_row, shift_by):
        return lax.dynamic_slice_in_dim(sample_row, shift_by, length)

    aligned = jax.vmap(take)(joined, delays[:, 0]).reshape(stn_here, frames_here, SPAN)
    own_spectra = spectrum(aligned, fringe)
    time_count = lax.axis_size("tm")
    channels_now = own_spectra.shape[3]
    cycle_size = lax.axis_size("stn")
    position = lax.axis_index("stn")
    totals = jnp.zeros((2, stn_here, stn_here * cycle_size, channels_now), jnp.float32)
    totals = place(totals, cross(own_spectra, own_spectra), position * stn_here)

    def turn_one(turn_index, state_tuple):
        current_totals, travel = state_tuple
        travel = passed_along(travel, "stn", 1)
        owner_index = (position - turn_index) % cycle_size
        current_totals = place(current_totals, cross(own_spectra, travel), owner_index * stn_here)
        return (current_totals, travel)

    totals, travel_end = lax.fori_loop(1, cycle_size, turn_one, (totals, own_spectra))
    norm_scale = 1.0 / jnp.sqrt(jnp.float32(frames_here * time_count))
    return lax.psum_scatter(totals * norm_scale, "tm", scatter_dimension=3, tiled=True)


def solution(mesh):
    return jax.shard_map(
        on_device,
        mesh=mesh,
        in_specs=(P(("band", "stn"), "tm"), P("stn", "tm"), P(("band", "stn"), "tm")),
        out_specs=P(None, ("band", "stn"), None, "tm"),
        check_vma=False,
    )
```

profile of v0, /device:TPU:0, one launch (start us, length us, event | category | flops | bytes accessed | tf_op | source)
XLA Modules:
  0.0 126.4 jit_solution(9294064870637160054)
XLA Ops:
  6.5 1.0 slice.55
  7.5 1.3 %collective-permute-start.1 = (bf16[1,24576]{1,0:T(2,128)(2,1)S(1)}, bf16[1,24576]{1,0:T(2,128)(2,1)S(1)}, u32[]{:S(2)}, u32[]{:S(2)}) collective-permute-start(bf16[1,24576]{1,0:T(2,128)(2,1)S(1)} %slice.55), channel_id=1, source_target_pairs={{1,0},{2,1},{3,2},{5,4},{6,5},{7,6},{9,8},{10,9},{11,10},{13,12},{... | collective-permute-start | bytes 147464 | tf_op jit(solution)/shard_map/ppermute | solution.py:13
  8.8 0.7 multiply_bitcast_fusion.1
  10.3 0.4 collective-permute-done.1
  10.7 3.7 %fusion.14 = bf16[131072]{0:T(1024)(128)(2,1)S(1)} fusion(s32[]{:T(128)} %bitcast.33, bf16[1,24576]{1,0:T(2,128)(2,1)S(1)} %collective-permute-done.1, bf16[1,131072]{1,0:T(2,128)(2,1)} %param.5), kind=kLoop, calls=%fused_computation.30 | loop fusion | flops 524288 | bytes 573444 | tf_op jit(solution)/shard_map/vmap()/gather | solution.py:95
  14.4 0.5 fusion.4
  14.9 0.5 convolution_bitcast_fusion
  15.4 1.7 %fusion.11 = f32[64,16,64]{2,0,1:T(8,128)S(1)} fusion(f32[64,1,16,128]{3,0,2,1:T(8,128)S(1)} %convolution_bitcast_fusion, f32[64,1,16,128]{3,0,2,1:T(8,128)S(1)} %fusion.4, f32[64,128]{1,0:T(8,128)S(1)} %get-tuple-element.171, f32[64,128]{1,0:T(8,128)S(1)} %get-tuple-element.172), kind=kOutput, calls=%fused_computation.25 | convolution fusion | flops 101171200 | bytes 1376256 | tf_op jit(solution)/shard_map/sfkb,bq->sfqk/dot_general | solution.py:58
  17.1 1.7 %fusion.9 = f32[64,16,64]{2,0,1:T(8,128)S(1)} fusion(f32[64,1,16,128]{3,0,2,1:T(8,128)S(1)} %fusion.4, f32[64,1,16,128]{3,0,2,1:T(8,128)S(1)} %convolution_bitcast_fusion, f32[64,128]{1,0:T(8,128)S(1)} %get-tuple-element.171, f32[64,128]{1,0:T(8,128)S(1)} %get-tuple-element.172), kind=kOutput, calls=%fused_computation.23 | convolution fusion | flops 101171200 | bytes 1376256 | tf_op jit(solution)/shard_map/sfkb,bq->sfqk/dot_general | solution.py:55
  18.8 1.7 %fusion.5 = f32[1,16,64,64]{3,2,1,0:T(8,128)S(1)} fusion(f32[64,16,64]{2,0,1:T(8,128)S(1)} %fusion.11, f32[64,1,16,128]{3,0,2,1:T(8,128)S(1)} %fusion.4, f32[64,1,16,128]{3,0,2,1:T(8,128)S(1)} %convolution_bitcast_fusion, f32[64,128]{1,0:T(8,128)S(1)} %get-tuple-element.171, f32[64,128]{1,0:T(8,128)S(1)} %get-tuple-element.172), kind=kOutput, calls=%fused_computation.16 | convolution fusion | flops 101236736 | bytes 1638400 | tf_op jit(solution)/shard_map/sfkb,bq->sfqk/dot_general | solution.py:58
  20.7 1.7 %fusion.6 = f32[1,16,64,64]{3,2,1,0:T(8,128)S(1)} fusion(f32[64,16,64]{2,0,1:T(8,128)S(1)} %fusion.9, f32[64,1,16,128]{3,0,2,1:T(8,128)S(1)} %convolution_bitcast_fusion, f32[64,1,16,128]{3,0,2,1:T(8,128)S(1)} %fusion.4, f32[64,128]{1,0:T(8,128)S(1)} %get-tuple-element.171, f32[64,128]{1,0:T(8,128)S(1)} %get-tuple-element.172), kind=kOutput, calls=%fused_computation.18 | convolution fusion | flops 101236736 | bytes 1638400 | tf_op jit(solution)/shard_map/sfkb,bq->sfqk/dot_general | solution.py:55
  23.0 0.5 dynamic_update_slice.13
  23.5 33.2 %while.18 = (s32[]{:T(128)}, f32[2,1,4,4096]{3,2,1,0:T(4,128)S(1)}, bf16[2,1,16,4096]{3,2,1,0:T(8,128)(2,1)S(1)}, s32[]{:T(128)}, bf16[2,1,16,4096]{3,2,1,0:T(8,...) while((s32[]{:T(128)}, f32[2,1,4,4096]{3,2,1,0:T(4,128)S(1)}, ...), condition=%wide.region_1.2_spmd, body=%wide.region_0.1_spmd.sunk | while | flops 794641 | bytes 2425128 | solution.py:113
  23.5 3.1 %collective-permute-start = (bf16[2,1,16,4096]{3,2,1,0:T(8,128)(2,1)S(1)}, bf16[2,1,16,4096]{3,2,1,0:T(8,128)(2,1)S(1)}, u32[]{:S(2)}, u32[]{:S(2)}) collective-permute-start(bf16[2,1,16,4096]{3,2,1,0:T(8,128)(2,1)S(1)} %get-tuple-element.223), channel_id=1, source_target_pairs={{0,4},{4,8},{8,12},{12,0},{1,5},{5,9},{9,13},{13,1},{2,6},{6,10},{... | collective-permute-start | bytes 786440 | tf_op jit(solution)/shard_map/while/body/eval_jaxpr/ppermute | solution.py:18
  26.6 7.2 %collective-permute-done = bf16[2,1,16,4096]{3,2,1,0:T(8,128)(2,1)S(1)} collective-permute-done((bf16[2,1,16,4096]{3,2,1,0:T(8,128)(2,1)S(1)}, bf16[2,1,16,4096]{3,2,1,0:T(8,128)(2,1)S(1)}, u32[]{:S(2)}, u32[]{:S(2)}) %collective-permute-start) | collective-permute-done | bytes 262176 | tf_op jit(solution)/shard_map/while/body/eval_jaxpr/ppermute | solution.py:18
  34.5 0.3 collective-permute-start
  34.8 9.9 %collective-permute-done = bf16[2,1,16,4096]{3,2,1,0:T(8,128)(2,1)S(1)} collective-permute-done((bf16[2,1,16,4096]{3,2,1,0:T(8,128)(2,1)S(1)}, bf16[2,1,16,4096]{3,2,1,0:T(8,128)(2,1)S(1)}, u32[]{:S(2)}, u32[]{:S(2)}) %collective-permute-start) | collective-permute-done | bytes 262176 | tf_op jit(solution)/shard_map/while/body/eval_jaxpr/ppermute | solution.py:18
  45.4 10.6 %collective-permute-done = bf16[2,1,16,4096]{3,2,1,0:T(8,128)(2,1)S(1)} collective-permute-done((bf16[2,1,16,4096]{3,2,1,0:T(8,128)(2,1)S(1)}, bf16[2,1,16,4096]{3,2,1,0:T(8,128)(2,1)S(1)}, u32[]{:S(2)}, u32[]{:S(2)}) %collective-permute-start) | collective-permute-done | bytes 262176 | tf_op jit(solution)/shard_map/while/body/eval_jaxpr/ppermute | solution.py:18
  56.8 6.9 %copy.58 = f32[2,1,4,4096]{2,1,0,3:T(1,128)} copy(f32[2,1,4,4096]{3,2,1,0:T(4,128)S(1)} %broadcast_multiply_fusion) | data formatting | bytes 262144
  63.7 16.7 %bitcast_reduce_fusion = f32[4096,2,4]{2,1,0:T(2,128)} fusion(f32[2,1,4,4096]{2,1,0,3:T(1,128)} %copy.58), kind=kLoop, calls=%fused_computation.11 | loop fusion | bytes 262144
  80.4 5.4 %reshape.458 = f32[4096,8]{1,0:T(8,128)} reshape(f32[4096,2,4]{2,1,0:T(2,128)} %bitcast_reduce_fusion) | data formatting | bytes 262144
  85.8 29.3 %reduce-scatter.4.cloned.1.call-done = f32[1024,8]{1,0:T(8,128)} async-done(((f32[4096,8]{1,0:T(8,128)}), f32[1024,8]{1,0:T(8,128)}) %reduce-scatter.4.cloned.1.call-update) | async-done | bytes 32784
  115.2 2.3 %reshape.459 = f32[1024,2,1,4]{3,2,1,0:T(1,128)S(1)} reshape(f32[1024,8]{1,0:T(8,128)} %reduce-scatter.4.cloned.1.call-done) | data formatting | bytes 65536
  117.4 2.1 %copy.59 = f32[2,1,4,1024]{3,2,1,0:T(4,128)} copy(f32[2,1,4,1024]{2,1,0,3:T(1,128)S(1)} %bitcast.133) | data formatting | bytes 65536
  (32 shorter events, 2.9 us)
Async XLA Ops:
  6.5 108.6 %reduce-scatter.4.cloned.1.call-start = ((), (), s32[]{:S(2)}) async-start(), calls=%async_computation.1 | async-start | bytes 2621440
  7.5 3.2 %collective-permute-start.1 = (bf16[1,24576]{1,0:T(2,128)(2,1)S(1)}, bf16[1,24576]{1,0:T(2,128)(2,1)S(1)}, u32[]{:S(2)}, u32[]{:S(2)}) collective-permute-start(bf16[1,24576]{1,0:T(2,128)(2,1)S(1)} %slice.55), channel_id=1, source_target_pairs={{1,0},{2,1},{3,2},{5,4},{6,5},{7,6},{9,8},{10,9},{11,10},{13,12},{... | collective-permute-start | bytes 147464 | tf_op jit(solution)/shard_map/ppermute | solution.py:13
  23.5 10.3 %collective-permute-start = (bf16[2,1,16,4096]{3,2,1,0:T(8,128)(2,1)S(1)}, bf16[2,1,16,4096]{3,2,1,0:T(8,128)(2,1)S(1)}, u32[]{:S(2)}, u32[]{:S(2)}) collective-permute-start(bf16[2,1,16,4096]{3,2,1,0:T(8,128)(2,1)S(1)} %get-tuple-element.223), channel_id=1, source_target_pairs={{0,4},{4,8},{8,12},{12,0},{1,5},{5,9},{9,13},{13,1},{2,6},{6,10},{... | collective-permute-start | bytes 786440 | tf_op jit(solution)/shard_map/while/body/eval_jaxpr/ppermute | solution.py:18
  34.5 10.2 %collective-permute-start = (bf16[2,1,16,4096]{3,2,1,0:T(8,128)(2,1)S(1)}, bf16[2,1,16,4096]{3,2,1,0:T(8,128)(2,1)S(1)}, u32[]{:S(2)}, u32[]{:S(2)}) collective-permute-start(bf16[2,1,16,4096]{3,2,1,0:T(8,128)(2,1)S(1)} %get-tuple-element.223), channel_id=1, source_target_pairs={{0,4},{4,8},{8,12},{12,0},{1,5},{5,9},{9,13},{13,1},{2,6},{6,10},{... | collective-permute-start | bytes 786440 | tf_op jit(solution)/shard_map/while/body/eval_jaxpr/ppermute | solution.py:18
  45.4 10.7 %collective-permute-start = (bf16[2,1,16,4096]{3,2,1,0:T(8,128)(2,1)S(1)}, bf16[2,1,16,4096]{3,2,1,0:T(8,128)(2,1)S(1)}, u32[]{:S(2)}, u32[]{:S(2)}) collective-permute-start(bf16[2,1,16,4096]{3,2,1,0:T(8,128)(2,1)S(1)} %get-tuple-element.223), channel_id=1, source_target_pairs={{0,4},{4,8},{8,12},{12,0},{1,5},{5,9},{9,13},{13,1},{2,6},{6,10},{... | collective-permute-start | bytes 786440 | tf_op jit(solution)/shard_map/while/body/eval_jaxpr/ppermute | solution.py:18
Sparse Core Ops, SparseCore 0:
  86.0 29.1 reduce-scatter.3
where the time goes:
time: 127 us; the launch traced here: 126 us
  waiting for transfers between devices  57.4 us (45%)
  local copies, waits for them, and re-layouts  36.3 us (29%)
  between operations  14.2 us (11%)
  matrix products  7.81 us (6%)
  other arithmetic  5.73 us (5%)
  starting transfers between devices  4.73 us (4%)
    unnamed x6, local copies, waits for them, and re-layouts  33.4 us
    unnamed x2, waiting for transfers between devices  29.3 us
    ppermute x3, waiting for transfers between devices, passed_along(): lax.ppermute(value, axis, [(i, (i + by) % size) for i in range(size)])  27.7 us
    gather x1, other arithmetic, take(): return lax.dynamic_slice_in_dim(sample_row, shift_by, length)  3.66 us
    ppermute x3, starting transfers between devices, passed_along(): lax.ppermute(value, axis, [(i, (i + by) % size) for i in range(size)])  3.44 us
  transfers between devices with their start and end apart: 5, of which 5 were waited for; matrix products, arithmetic and copies ran while one was open for 1% of the time, Pallas kernels for 0%

commit v1 on v0

--- a/solution.py
+++ b/solution.py
@@ -1,8 +1,16 @@
+import functools
+import math
+
 import jax
 import jax.numpy as jnp
+import ml_dtypes
+import numpy as np
 from jax import lax
+from jax.experimental import pallas as pl
+from jax.experimental.pallas import tpu as pltpu
 from jax.sharding import PartitionSpec as P
 
+MESH = pl.DeviceIdType.MESH
 SPAN = 8192
 DMAX = 24576
 
@@ -115,9 +123,273 @@
     return lax.psum_scatter(totals * norm_scale, "tm", scatter_dimension=3, tiled=True)
 
 
+LANES = 128
+CHUNK = 4
+
+
+def spectrum_tables(stn_count, tm_count):
+    first = np.arange(64)
+    second = np.arange(LANES)
+    turn = 2.0 * np.pi * (first[:, None] * first[None, :] % 64) / 64.0
+    first_table = np.concatenate([np.cos(turn), -np.sin(turn)], axis=0)
+    twist = 2.0 * np.pi * (first[:, None] * second[None, :]) / SPAN
+    twist_table = np.stack([np.cos(twist), -np.sin(twist)]) / np.sqrt(SPAN)
+    rows = []
+    for block in range(stn_count * tm_count):
+        q = block * 4 + np.array([0, 2, 1, 3])
+        turn = 2.0 * np.pi * (q[:, None] * second[None, :] % LANES) / LANES
+        rows.append(np.concatenate([np.cos(turn), np.sin(turn)], axis=1))
+        rows.append(np.concatenate([-np.sin(turn), np.cos(turn)], axis=1))
+    second_table = np.concatenate(rows, axis=0)
+
+    def halves(table):
+        high = table.astype(ml_dtypes.bfloat16)
+        return high, (table - high.astype(np.float64)).astype(ml_dtypes.bfloat16)
+
+    first_table = np.concatenate(halves(first_table), axis=1)
+    second_table = np.concatenate(halves(second_table), axis=0)
+    return first_table, twist_table.astype(np.float32), second_table
+
+
+def fused_kernel(
+    S, T, norm_scale,
+    samples_ref, delays_ref, fringe_ref, first_ref, twist_ref, second_ref,
+    out_ref,
+    tail, outgoing, incoming, pieces, landed,
+    halo_sems, send_sems, recv_sems, last_send_sems, last_recv_sems,
+):
+    f32, bf16 = jnp.float32, jnp.bfloat16
+    band = lax.axis_index("band")
+    s_me = lax.axis_index("stn")
+    t_me = lax.axis_index("tm")
+    partners = [(ds, dt) for ds in (2, 3, 1, 0) for dt in range(T) if (ds, dt) != (0, 0)]
+    rows_chunk = CHUNK * 64
+    chunks = samples_ref.shape[0] // rows_chunk
+    halo_rows = DMAX // LANES
+    tail_start = (chunks - 1) * rows_chunk
+
+    def partner(ds, dt):
+        return lax.rem(s_me + ds, S), lax.rem(t_me + dt, T)
+
+    barrier = pltpu.get_barrier_semaphore()
+    for ds, dt in partners:
+        s_to, t_to = partner(ds, dt)
+        pl.semaphore_signal(barrier, inc=1, device_id=(band, s_to, t_to), device_id_type=MESH)
+
+    tail[pl.ds(0, rows_chunk), :] = samples_ref[pl.ds(tail_start, rows_chunk), :]
+    tail[pl.ds(rows_chunk + halo_rows, 8), :] = jnp.zeros((8, LANES), f32)
+
+    @pl.when(t_me == T - 1)
+    def _():
+        tail[pl.ds(rows_chunk, halo_rows), :] = jnp.zeros((halo_rows, LANES), f32)
+
+    delay = delays_ref[0, 0]
+    delay_rows = delay // LANES
+    delay_lanes = delay - delay_rows * LANES
+    lane_from = lax.broadcasted_iota(jnp.int32, (2 * LANES, LANES), 0)
+    lane_to = lax.broadcasted_iota(jnp.int32, (2 * LANES, LANES), 1)
+    shift = jnp.where(lane_from == lane_to + delay_lanes, 1.0, 0.0).astype(bf16)
+
+    phase = fringe_ref[...].astype(f32) * (2.0 * math.pi / 65536.0)
+    cos_fringe = jnp.cos(phase)
+    sin_fringe = jnp.sin(phase)
+
+    def chunk_spectra(c):
+        source, start = (tail, 0) if c == chunks - 1 else (samples_ref, c * rows_chunk)
+        here = source[pl.ds(delay_rows + start, rows_chunk), :].astype(bf16)
+        after = source[pl.ds(delay_rows + (start + 1), rows_chunk), :].astype(bf16)
+        aligned = jnp.dot(
+            jnp.concatenate([here, after], axis=1), shift, preferred_element_type=f32
+        ).astype(bf16)
+        frames = [aligned[64 * f : 64 * (f + 1)] for f in range(CHUNK)]
+        side = jnp.concatenate(frames, axis=1)
+        first = jnp.dot(
+            first_ref[...], jnp.concatenate([side, side], axis=0), preferred_element_type=f32
+        )
+        twisted = []
+        for f in range(CHUNK):
+            at = c * CHUNK + f
+            cos_f = cos_fringe[:, at : at + 1]
+            sin_f = sin_fringe[:, at : at + 1]
+            twist_real = twist_ref[0] * cos_f + twist_ref[1] * sin_f
+            twist_imag = twist_ref[1] * cos_f - twist_ref[0] * sin_f
+            real = first[:64, LANES * f : LANES * (f + 1)]
+            imag = first[64:, LANES * f : LANES * (f + 1)]
+            twisted.append(
+                jnp.concatenate(
+                    [
+                        real * twist_real - imag * twist_imag,
+                        real * twist_imag + imag * twist_real,
+                    ],
+                    axis=1,
+                )
+            )
+        twisted = jnp.concatenate(twisted, axis=0)
+        high = twisted.astype(bf16)
+        low = (twisted - high.astype(f32)).astype(bf16)
+        across = (((1,), (1,)), ((), ()))
+        both = lax.dot_general(second_ref[...], high, across, preferred_element_type=f32)
+        small = lax.dot_general(second_ref[:LANES], low, across, preferred_element_type=f32)
+        spectra = both[:LANES] + (both[LANES:] + small)
+        blocks = jnp.concatenate(
+            [
+                spectra[:, :LANES].reshape(S * T, 8, LANES),
+                spectra[:, LANES:].reshape(S * T, 8, LANES),
+            ],
+            axis=1,
+        )
+        outgoing[c] = blocks.astype(bf16)
+
+    def spectra_copy(c, ds, dt):
+        s_to, t_to = partner(ds, dt)
+        return pltpu.make_async_remote_copy(
+            src_ref=outgoing.at[c, t_to * S + s_to],
+            dst_ref=incoming.at[c, s_me, dt],
+            send_sem=send_sems.at[c, ds, dt],
+            recv_sem=recv_sems.at[c, ds, dt],
+            device_id=(band, s_to, t_to),
+            device_id_type=MESH,
+        )
+
+    def halo_copy():
+        return pltpu.make_async_remote_copy(
+            src_ref=samples_ref.at[pl.ds(0, halo_rows)],
+            dst_ref=tail.at[pl.ds(rows_chunk, halo_rows)],
+            send_sem=halo_sems.at[0],
+            recv_sem=halo_sems.at[1],
+            device_id=(band, s_me, lax.rem(t_me + T - 1, T)),
+            device_id_type=MESH,
+        )
+
+    for c in range(chunks):
+        if c == chunks - 1:
+
+            @pl.when(t_me < T - 1)
+            def _():
+                halo_copy().wait_recv()
+
+        chunk_spectra(c)
+        if c == 0:
+            pl.semaphore_wait(barrier, len(partners))
+
+            @pl.when(t_me > 0)
+            def _():
+                halo_copy().start()
+
+        for ds, dt in partners:
+            spectra_copy(c, ds, dt).start()
+        incoming[c, s_me, 0] = outgoing[c, t_me * S + s_me]
+
+    pairs = [(i, j) for i in range(S) for j in range(i, S)]
+    even = {pair: jnp.zeros((8, LANES), f32) for pair in pairs}
+    odd = {pair: jnp.zeros((8, LANES), f32) for pair in pairs if pair[0] != pair[1]}
+    for c in range(chunks):
+        for ds, dt in partners:
+            spectra_copy(c, ds, dt).wait_recv()
+        for dt in range(T):
+            tiles = [incoming[c, s, dt].astype(f32) for s in range(S)]
+            for half in range(2):
+                part = [tile[8 * half : 8 * half + 8] for tile in tiles]
+                turned = [None] + [pltpu.roll(p, 4, 0) for p in part[1:]]
+                for i, j in pairs:
+                    even[i, j] += part[i] * part[j]
+                    if i != j:
+                        odd[i, j] += part[i] * turned[j]
+
+    left = lax.broadcasted_iota(jnp.int32, (8, LANES), 1) < 64
+
+    def settle(total, sign):
+        total = total + pltpu.roll(total, 64, 1)
+        total = (pltpu.roll(total, 4, 0) + sign * total) * norm_scale
+        return jnp.where(left, total, pltpu.roll(total, 6, 0))
+
+    def put(i, row, value):
+        pieces[i, pl.ds(row, 1), pl.ds(0, LANES)] = value[0:1]
+        pieces[i, pl.ds(row, 1), pl.ds(LANES, LANES)] = value[1:2]
+
+    for i, j in pairs:
+        real = settle(even[i, j], 1.0)
+        put(i, j, real)
+        if i == j:
+            put(i, S + i, jnp.zeros_like(real))
+        else:
+            put(j, i, real)
+            imag = settle(odd[i, j], -1.0)
+            put(i, S + j, imag)
+            put(j, S + i, -imag)
+
+    def last_copy(ds):
+        s_to = lax.rem(s_me + ds, S)
+        return pltpu.make_async_remote_copy(
+            src_ref=pieces.at[s_to],
+            dst_ref=landed.at[s_me],
+            send_sem=last_send_sems.at[ds],
+            recv_sem=last_recv_sems.at[ds],
+            device_id=(band, s_to, t_me),
+            device_id_type=MESH,
+        )
+
+    for ds in (2, 3, 1):
+        last_copy(ds).start()
+    landed[s_me] = pieces[s_me]
+    for ds in (2, 3, 1):
+        last_copy(ds).wait_recv()
+    for s in range(S):
+        out_ref[:, pl.ds(s * 2 * LANES, 2 * LANES)] = landed[s]
+
+    for ds in (2, 3, 1):
+        last_copy(ds).wait_send()
+    for c in range(chunks):
+        for ds, dt in partners:
+            spectra_copy(c, ds, dt).wait_send()
+
+    @pl.when(t_me > 0)
+    def _():
+        halo_copy().wait_send()
+
+
+def fused_on_device(stn_count, tm_count, samples, delays, fringe):
+    length = samples.shape[1]
+    rows = length // LANES
+    chunks = rows // (CHUNK * 64)
+    blocks = stn_count * tm_count
+    signal = samples.astype(jnp.float32).reshape(rows, LANES)
+    first_table, twist_table, second_table = spectrum_tables(stn_count, tm_count)
+    norm_scale = 1.0 / math.sqrt(length // SPAN * tm_count)
+    vmem = pl.BlockSpec(memory_space=pltpu.VMEM)
+    smem = pl.BlockSpec(memory_space=pltpu.SMEM)
+    out = pl.pallas_call(
+        functools.partial(fused_kernel, stn_count, tm_count, norm_scale),
+        out_shape=jax.ShapeDtypeStruct((2 * stn_count, 1024), jnp.float32),
+        in_specs=[vmem, smem, vmem, vmem, vmem, vmem],
+        out_specs=vmem,
+        scratch_shapes=[
+            pltpu.VMEM((CHUNK * 64 + DMAX // LANES + 8, LANES), jnp.float32),
+            pltpu.VMEM((chunks, blocks, 16, LANES), jnp.bfloat16),
+            pltpu.VMEM((chunks, stn_count, tm_count, 16, LANES), jnp.bfloat16),
+            pltpu.VMEM((stn_count, 2 * stn_count, 2 * LANES), jnp.float32),
+            pltpu.VMEM((stn_count, 2 * stn_count, 2 * LANES), jnp.float32),
+            pltpu.SemaphoreType.DMA((2,)),
+            pltpu.SemaphoreType.DMA((chunks, stn_count, tm_count)),
+            pltpu.SemaphoreType.DMA((chunks, stn_count, tm_count)),
+            pltpu.SemaphoreType.DMA((stn_count,)),
+            pltpu.SemaphoreType.DMA((stn_count,)),
+        ],
+        compiler_params=pltpu.CompilerParams(
+            collective_id=0, has_side_effects=True, vmem_limit_bytes=32 << 20
+        ),
+        name="correlate",
+    )(signal, delays, fringe, jnp.asarray(first_table), jnp.asarray(twist_table), jnp.asarray(second_table))
+    return out.reshape(2, 1, stn_count, 1024)
+
+
 def solution(mesh):
+    stn_count, tm_count = mesh.shape["stn"], mesh.shape["tm"]
+    body = on_device
+    if (stn_count, tm_count) == (4, 4):
+        body = functools.partial(fused_on_device, stn_count, tm_count)
     return jax.shard_map(
-        on_device,
+        body,
         mesh=mesh,
         in_specs=(P(("band", "stn"), "tm"), P("stn", "tm"), P(("band", "stn"), "tm")),
         out_specs=P(None, ("band", "stn"), None, "tm"),

time: 127 us -> 23.2 us (0.18)
  waiting for transfers between devices: 57.4 us -> 0 us
  local copies, waits for them, and re-layouts: 36.3 us -> 1.27 us
  Pallas kernels: 0 us -> 19.5 us
  between operations: 14.2 us -> 0.72 us
  matrix products: 7.81 us -> 0 us
  starting transfers between devices: 4.73 us -> 0 us
  other arithmetic: 5.73 us -> 1.63 us
    unnamed x6 -> x8, local copies, waits for them, and re-layouts: 33.4 us -> 0.64 us
    unnamed x2 -> x0, waiting for transfers between devices: 29.3 us -> none
    ppermute x4 -> x0, waiting for transfers between devices: 28.1 us -> none  [the longest x3 27.7 us: passed_along(): lax.ppermute(value, axis, [(i, (i + by) % size) for i in range(size)])]
    pallas_call x0 -> x1, Pallas kernels: none -> 19.5 us  [fused_on_device(): pl.pallas_call(functools.partial(fused_kernel, stn_count, tm_count, norm_...]
    dot_general x6 -> x0, matrix products: 7.81 us -> none  [the longest x1 1.72 us: spectrum(): jnp.einsum('sfkb,bq->sfqk', twist_real, sin_second, precision=high)]
    ppermute x4 -> x0, starting transfers between devices: 4.73 us -> none  [the longest x3 3.44 us: passed_along(): lax.ppermute(value, axis, [(i, (i + by) % size) for i in range(size)])]
    gather x1 -> x0, other arithmetic: 3.66 us -> none  [take(): return lax.dynamic_slice_in_dim(sample_row, shift_by, length)]
    reshape x0 -> x1, other arithmetic: none -> 1.63 us  [fused_on_device(): signal = samples.astype(jnp.float32).reshape(rows, LANES)]
  transfers between devices with their start and end apart: 5 -> 0, of which waited for: 5 -> 0; matrix products, arithmetic and copies ran while one was open for 1% -> 0% of each run, Pallas kernels for 0% -> 0%
where the time goes in v1:
time: 23.2 us; the launch traced here: 23.1 us
  Pallas kernels  19.5 us (84%)
  other arithmetic  1.63 us (7%)
  local copies, waits for them, and re-layouts  1.27 us (5%)
  between operations  0.72 us (3%)
    pallas_call x1, Pallas kernels, fused_on_device(): pl.pallas_call(functools.partial(fused_kernel, stn_count, tm_count, norm_...  19.5 us
    reshape x1, other arithmetic, fused_on_device(): signal = samples.astype(jnp.float32).reshape(rows, LANES)  1.63 us
    unnamed x8, local copies, waits for them, and re-layouts  0.64 us
    reshape x1, local copies, waits for them, and re-layouts, fused_on_device(): return out.reshape(2, 1, stn_count, 1024)  0.63 us

profile of v1, /device:TPU:0, one launch (start us, length us, event | category | flops | bytes accessed | tf_op | source)
XLA Modules:
  0.0 23.1 jit_solution(2573224969453929070)
XLA Ops:
  0.7 0.0 copy-start
  0.7 0.0 copy-start.1
  0.7 0.0 copy-start.2
  0.7 1.6 %reshape.11 = f32[1,131072]{1,0:T(1,128)S(1)} convert(bf16[1,131072]{1,0:T(2,128)(2,1)} %param.6) | non-fusion elementwise | flops 131072 | bytes 786432 | tf_op jit(solution)/shard_map/reshape | solution.py:356
  2.3 0.0 copy-start.3
  2.3 0.0 copy-done
  2.3 0.0 copy-done.1
  2.4 0.0 copy-done.2
  2.4 0.6 %copy-done.3 = s32[1,16]{1,0:T(1,128)S(1)} copy-done((s32[1,16]{1,0:T(1,128)S(1)}, s32[1,16]{1,0:T(1,128)}, u32[]{:S(2)}) %copy-start.3) | copy-done | bytes 88
  3.0 19.5 %correlate.1 = f32[8,1024]{1,0:T(8,128)S(1)} custom-call(f32[1024,128]{1,0:T(8,128)S(1)} %bitcast.2, s32[1,1]{1,0:T(1,128)S(6)} %copy.8.delays_ref, s32[1,16]{1,0:T(1,128)S(1)} %copy-done.3, bf16[128,128]{1,0:T(8,128)(2,1)S(1)} %copy-done.2, f32[2,64,128]{2,1,0:T(8,128)S(1)} %copy-done.1, bf16[256,256]{1,0:T(8,128)(2,1)S(1)} %copy-done), custom_call_target="tpu_custom_call" | custom-call | tf_op jit(solution)/shard_map/correlate/pallas_call | solution.py:361
  22.5 0.6 %reshape.10 = f32[2,1,4,1024]{3,2,0,1:T(4,128)} reshape(f32[8,1024]{1,0:T(8,128)S(1)} %correlate.1) | data formatting | bytes 65536 | tf_op jit(solution)/shard_map/reshape | solution.py:383
Async XLA Ops:
  0.7 1.7 %copy-start = (bf16[256,256]{1,0:T(8,128)(2,1)S(1)}, bf16[256,256]{1,0:T(8,128)(2,1)}, u32[]{:S(2)}) copy-start(bf16[256,256]{1,0:T(8,128)(2,1)} %constant.8.clone.second_ref) | copy-start | bytes 393220
  0.7 1.7 %copy-start.1 = (f32[2,64,128]{2,1,0:T(8,128)S(1)}, f32[2,64,128]{2,1,0:T(8,128)}, u32[]{:S(2)}) copy-start(f32[2,64,128]{2,1,0:T(8,128)} %constant.7.clone.twist_ref) | copy-start | bytes 196612
  0.7 1.7 %copy-start.2 = (bf16[128,128]{1,0:T(8,128)(2,1)S(1)}, bf16[128,128]{1,0:T(8,128)(2,1)}, u32[]{:S(2)}) copy-start(bf16[128,128]{1,0:T(8,128)(2,1)} %constant.6.clone.first_ref) | copy-start | bytes 98308
  2.3 0.7 %copy-start.3 = (s32[1,16]{1,0:T(1,128)S(1)}, s32[1,16]{1,0:T(1,128)}, u32[]{:S(2)}) copy-start(s32[1,16]{1,0:T(1,128)} %fringe_ref.1) | copy-start | bytes 196

commit v2 on v1

--- a/solution.py
+++ b/solution.py
@@ -125,6 +125,7 @@
 
 LANES = 128
 CHUNK = 4
+GROUPS = ((0, 0), (1, 1), (2, 2), (3, 3))
 
 
 def spectrum_tables(stn_count, tm_count):
@@ -153,10 +154,11 @@
 
 def fused_kernel(
     S, T, norm_scale,
-    samples_ref, delays_ref, fringe_ref, first_ref, twist_ref, second_ref,
+    samples_hbm, delays_hbm, fringe_hbm, first_hbm, twist_hbm, second_hbm,
     out_ref,
-    tail, outgoing, incoming, pieces, landed,
-    halo_sems, send_sems, recv_sems, last_send_sems, last_recv_sems,
+    flat, delays_ref, fringe_ref, first_ref, twist_ref, second_ref,
+    signal, tail, outgoing, incoming, pieces, landed,
+    load_sems, halo_sems, send_sem, recv_sems, last_sems,
 ):
     f32, bf16 = jnp.float32, jnp.bfloat16
     band = lax.axis_index("band")
@@ -164,25 +166,54 @@
     t_me = lax.axis_index("tm")
     partners = [(ds, dt) for ds in (2, 3, 1, 0) for dt in range(T) if (ds, dt) != (0, 0)]
     rows_chunk = CHUNK * 64
-    chunks = samples_ref.shape[0] // rows_chunk
+    chunks = signal.shape[0] // rows_chunk
     halo_rows = DMAX // LANES
     tail_start = (chunks - 1) * rows_chunk
 
     def partner(ds, dt):
         return lax.rem(s_me + ds, S), lax.rem(t_me + dt, T)
+
+    half = flat.shape[1] // 2
+    loads = [
+        pltpu.make_async_copy(source, target, load_sems.at[index])
+        for index, (source, target) in enumerate(
+            [
+                (samples_hbm.at[:, pl.ds(0, half)], flat.at[:, pl.ds(0, half)]),
+                (delays_hbm, delays_ref),
+                (first_hbm, first_ref),
+                (fringe_hbm, fringe_ref),
+                (twist_hbm, twist_ref),
+                (second_hbm, second_ref),
+                (samples_hbm.at[:, pl.ds(half, half)], flat.at[:, pl.ds(half, half)]),
+            ]
+        )
+    ]
+    for load in loads:
+        load.start()
 
     barrier = pltpu.get_barrier_semaphore()
     for ds, dt in partners:
         s_to, t_to = partner(ds, dt)
         pl.semaphore_signal(barrier, inc=1, device_id=(band, s_to, t_to), device_id_type=MESH)
 
-    tail[pl.ds(0, rows_chunk), :] = samples_ref[pl.ds(tail_start, rows_chunk), :]
     tail[pl.ds(rows_chunk + halo_rows, 8), :] = jnp.zeros((8, LANES), f32)
 
     @pl.when(t_me == T - 1)
     def _():
         tail[pl.ds(rows_chunk, halo_rows), :] = jnp.zeros((halo_rows, LANES), f32)
 
+    def lay_out(first_row, row_count):
+        for row in range(first_row, first_row + row_count, 64):
+            part = flat[:, pl.ds(row * LANES, 64 * LANES)].astype(f32).reshape(64, LANES)
+            signal[pl.ds(row, 64), :] = part
+            if row >= tail_start:
+                tail[pl.ds(row - tail_start, 64), :] = part
+
+    loads[0].wait()
+    lay_out(0, 2 * rows_chunk)
+    loads[1].wait()
+    loads[2].wait()
+    loads[3].wait()
     delay = delays_ref[0, 0]
     delay_rows = delay // LANES
     delay_lanes = delay - delay_rows * LANES
@@ -195,7 +226,7 @@
     sin_fringe = jnp.sin(phase)
 
     def chunk_spectra(c):
-        source, start = (tail, 0) if c == chunks - 1 else (samples_ref, c * rows_chunk)
+        source, start = (tail, 0) if c == chunks - 1 else (signal, c * rows_chunk)
         here = source[pl.ds(delay_rows + start, rows_chunk), :].astype(bf16)
         after = source[pl.ds(delay_rows + (start + 1), rows_chunk), :].astype(bf16)
         aligned = jnp.dot(
@@ -231,29 +262,35 @@
         both = lax.dot_general(second_ref[...], high, across, preferred_element_type=f32)
         small = lax.dot_general(second_ref[:LANES], low, across, preferred_element_type=f32)
         spectra = both[:LANES] + (both[LANES:] + small)
-        blocks = jnp.concatenate(
+        outgoing[:, c] = jnp.concatenate(
             [
                 spectra[:, :LANES].reshape(S * T, 8, LANES),
                 spectra[:, LANES:].reshape(S * T, 8, LANES),
             ],
             axis=1,
-        )
-        outgoing[c] = blocks.astype(bf16)
-
-    def spectra_copy(c, ds, dt):
+        ).astype(bf16)
+
+    def spectra_copy(group, ds, dt):
         s_to, t_to = partner(ds, dt)
+        first_chunk, last_chunk = GROUPS[group]
+        part = pl.ds(first_chunk, last_chunk + 1 - first_chunk)
         return pltpu.make_async_remote_copy(
-            src_ref=outgoing.at[c, t_to * S + s_to],
-            dst_ref=incoming.at[c, s_me, dt],
-            send_sem=send_sems.at[c, ds, dt],
-            recv_sem=recv_sems.at[c, ds, dt],
+            src_ref=outgoing.at[t_to * S + s_to, part],
+            dst_ref=incoming.at[s_me * T + dt, part],
+            send_sem=send_sem,
+            recv_sem=recv_sems.at[group],
             device_id=(band, s_to, t_to),
             device_id_type=MESH,
         )
 
+    def all_arrived(group):
+        first_chunk, last_chunk = GROUPS[group]
+        part = incoming.at[pl.ds(0, S * T - 1), pl.ds(first_chunk, last_chunk + 1 - first_chunk)]
+        pltpu.make_async_copy(part, part, recv_sems.at[group]).wait()
+
     def halo_copy():
         return pltpu.make_async_remote_copy(
-            src_ref=samples_ref.at[pl.ds(0, halo_rows)],
+            src_ref=signal.at[pl.ds(0, halo_rows)],
             dst_ref=tail.at[pl.ds(rows_chunk, halo_rows)],
             send_sem=halo_sems.at[0],
             recv_sem=halo_sems.at[1],
@@ -262,7 +299,15 @@
         )
 
     for c in range(chunks):
-        if c == chunks - 1:
+        if c == 0:
+            loads[4].wait()
+            loads[5].wait()
+        elif c == 1:
+            loads[6].wait()
+            lay_out(2 * rows_chunk, rows_chunk)
+        elif c == 2:
+            lay_out(3 * rows_chunk, rows_chunk)
+        else:
 
             @pl.when(t_me < T - 1)
             def _():
@@ -276,20 +321,21 @@
             def _():
                 halo_copy().start()
 
-        for ds, dt in partners:
-            spectra_copy(c, ds, dt).start()
-        incoming[c, s_me, 0] = outgoing[c, t_me * S + s_me]
+        for group, (_, last_chunk) in enumerate(GROUPS):
+            if last_chunk == c:
+                for ds, dt in partners:
+                    spectra_copy(group, ds, dt).start()
+        incoming[s_me * T, c] = outgoing[t_me * S + s_me, c]
 
     pairs = [(i, j) for i in range(S) for j in range(i, S)]
     even = {pair: jnp.zeros((8, LANES), f32) for pair in pairs}
     odd = {pair: jnp.zeros((8, LANES), f32) for pair in pairs if pair[0] != pair[1]}
-    for c in range(chunks):
-        for ds, dt in partners:
-            spectra_copy(c, ds, dt).wait_recv()
-        for dt in range(T):
-            tiles = [incoming[c, s, dt].astype(f32) for s in range(S)]
-            for half in range(2):
-                part = [tile[8 * half : 8 * half + 8] for tile in tiles]
+    for group, (first_chunk, last_chunk) in enumerate(GROUPS):
+        all_arrived(group)
+        for dt, c in [(dt, c) for dt in range(T) for c in range(first_chunk, last_chunk + 1)]:
+            tiles = [incoming[s * T + dt, c].astype(f32) for s in range(S)]
+            for top in (0, 8):
+                part = [tile[top : top + 8] for tile in tiles]
                 turned = [None] + [pltpu.roll(p, 4, 0) for p in part[1:]]
                 for i, j in pairs:
                     even[i, j] += part[i] * part[j]
@@ -323,8 +369,8 @@
         return pltpu.make_async_remote_copy(
             src_ref=pieces.at[s_to],
             dst_ref=landed.at[s_me],
-            send_sem=last_send_sems.at[ds],
-            recv_sem=last_recv_sems.at[ds],
+            send_sem=last_sems.at[0],
+            recv_sem=last_sems.at[1],
             device_id=(band, s_to, t_me),
             device_id_type=MESH,
         )
@@ -332,16 +378,14 @@
     for ds in (2, 3, 1):
         last_copy(ds).start()
     landed[s_me] = pieces[s_me]
-    for ds in (2, 3, 1):
-        last_copy(ds).wait_recv()
+    others = landed.at[pl.ds(0, S - 1)]
+    pltpu.make_async_copy(others, others, last_sems.at[1]).wait()
     for s in range(S):
         out_ref[:, pl.ds(s * 2 * LANES, 2 * LANES)] = landed[s]
 
-    for ds in (2, 3, 1):
-        last_copy(ds).wait_send()
-    for c in range(chunks):
-        for ds, dt in partners:
-            spectra_copy(c, ds, dt).wait_send()
+    pltpu.make_async_copy(others, others, last_sems.at[0]).wait()
+    sent = outgoing.at[pl.ds(0, S * T - 1)]
+    pltpu.make_async_copy(sent, sent, send_sem).wait()
 
     @pl.when(t_me > 0)
     def _():
@@ -353,33 +397,37 @@
     rows = length // LANES
     chunks = rows // (CHUNK * 64)
     blocks = stn_count * tm_count
-    signal = samples.astype(jnp.float32).reshape(rows, LANES)
-    first_table, twist_table, second_table = spectrum_tables(stn_count, tm_count)
     norm_scale = 1.0 / math.sqrt(length // SPAN * tm_count)
-    vmem = pl.BlockSpec(memory_space=pltpu.VMEM)
-    smem = pl.BlockSpec(memory_space=pltpu.SMEM)
+    tables = spectrum_tables(stn_count, tm_count)
+    operands = [samples, delays, fringe] + [jnp.asarray(table) for table in tables]
     out = pl.pallas_call(
         functools.partial(fused_kernel, stn_count, tm_count, norm_scale),
         out_shape=jax.ShapeDtypeStruct((2 * stn_count, 1024), jnp.float32),
-        in_specs=[vmem, smem, vmem, vmem, vmem, vmem],
-        out_specs=vmem,
+        in_specs=[pl.BlockSpec(memory_space=pltpu.HBM)] * len(operands),
+        out_specs=pl.BlockSpec(memory_space=pltpu.VMEM),
         scratch_shapes=[
+            pltpu.VMEM(samples.shape, samples.dtype),
+            pltpu.SMEM(delays.shape, delays.dtype),
+        ]
+        + [pltpu.VMEM(operand.shape, operand.dtype) for operand in operands[2:]]
+        + [
+            pltpu.VMEM((rows, LANES), jnp.float32),
             pltpu.VMEM((CHUNK * 64 + DMAX // LANES + 8, LANES), jnp.float32),
-            pltpu.VMEM((chunks, blocks, 16, LANES), jnp.bfloat16),
-            pltpu.VMEM((chunks, stn_count, tm_count, 16, LANES), jnp.bfloat16),
+            pltpu.VMEM((blocks, chunks, 16, LANES), jnp.bfloat16),
+            pltpu.VMEM((blocks, chunks, 16, LANES), jnp.bfloat16),
             pltpu.VMEM((stn_count, 2 * stn_count, 2 * LANES), jnp.float32),
             pltpu.VMEM((stn_count, 2 * stn_count, 2 * LANES), jnp.float32),
+            pltpu.SemaphoreType.DMA((7,)),
             pltpu.SemaphoreType.DMA((2,)),
-            pltpu.SemaphoreType.DMA((chunks, stn_count, tm_count)),
-            pltpu.SemaphoreType.DMA((chunks, stn_count, tm_count)),
-            pltpu.SemaphoreType.DMA((stn_count,)),
-            pltpu.SemaphoreType.DMA((stn_count,)),
+            pltpu.SemaphoreType.DMA,
+            pltpu.SemaphoreType.DMA((len(GROUPS),)),
+            pltpu.SemaphoreType.DMA((2,)),
         ],
         compiler_params=pltpu.CompilerParams(
-            collective_id=0, has_side_effects=True, vmem_limit_bytes=32 << 20
+            collective_id=0, has_side_effects=True, vmem_limit_bytes=60 << 20
         ),
         name="correlate",
-    )(signal, delays, fringe, jnp.asarray(first_table), jnp.asarray(twist_table), jnp.asarray(second_table))
+    )(*operands)
     return out.reshape(2, 1, stn_count, 1024)
 
 

time: 23.2 us -> 21.4 us (0.922)
  other arithmetic: 1.63 us -> 0 us
  Pallas kernels: 19.5 us -> 19.2 us
    reshape x1 -> x0, other arithmetic: 1.63 us -> none  [fused_on_device(): signal = samples.astype(jnp.float32).reshape(rows, LANES)]
    reshape x1, local copies, waits for them, and re-layouts: 0.63 us -> 1.39 us  [fused_on_device(): return out.reshape(2, 1, stn_count, 1024)]
    unnamed x8 -> x0, local copies, waits for them, and re-layouts: 0.64 us -> none
    pallas_call x1, Pallas kernels: 19.5 us -> 19.2 us  [fused_on_device(): pl.pallas_call(functools.partial(fused_kernel, stn_count, tm_count, norm_...]
where the time goes in v2:
time: 21.4 us; the launch traced here: 21.2 us
  Pallas kernels  19.2 us (90%)
  local copies, waits for them, and re-layouts  1.39 us (6%)
  between operations  0.66 us (3%)
    pallas_call x1, Pallas kernels, fused_on_device(): pl.pallas_call(functools.partial(fused_kernel, stn_count, tm_count, norm_...  19.2 us
    reshape x1, local copies, waits for them, and re-layouts, fused_on_device(): return out.reshape(2, 1, stn_count, 1024)  1.39 us

profile of v2, /device:TPU:0, one launch (start us, length us, event | category | flops | bytes accessed | tf_op | source)
XLA Modules:
  0.0 21.2 jit_solution(3005647905957265906)
XLA Ops:
  0.7 19.2 %correlate.1 = f32[8,1024]{1,0:T(8,128)} custom-call(bf16[1,131072]{1,0:T(2,128)(2,1)} %samples_hbm.1, s32[1,1]{1,0:T(1,128)S(6)} %copy.8.delays_hbm, s32[1,16]{1,0:T(1,128)} %fringe_hbm.1, bf16[128,128]{1,0:T(8,128)(2,1)} %constant.6.clone.first_hbm, f32[2,64,128]{2,1,0:T(8,128)} %constant.7.clone.twist_hbm, bf16[256,256]{1,0:T(8,128)(2,1)} %constant.8.clone.second_hbm), custom_call_target="tpu_custom_call" | custom-call | tf_op jit(solution)/shard_map/correlate/pallas_call | solution.py:403
  19.8 1.4 %reshape.3 = f32[2,1,4,1024]{3,2,0,1:T(4,128)} reshape(f32[8,1024]{1,0:T(8,128)} %correlate.1) | data formatting | bytes 65536 | tf_op jit(solution)/shard_map/reshape | solution.py:431

commit v3 on v2

--- a/solution.py
+++ b/solution.py
@@ -125,7 +125,6 @@
 
 LANES = 128
 CHUNK = 4
-GROUPS = ((0, 0), (1, 1), (2, 2), (3, 3))
 
 
 def spectrum_tables(stn_count, tm_count):
@@ -157,21 +156,17 @@
     samples_hbm, delays_hbm, fringe_hbm, first_hbm, twist_hbm, second_hbm,
     out_ref,
     flat, delays_ref, fringe_ref, first_ref, twist_ref, second_ref,
-    signal, tail, outgoing, incoming, pieces, landed,
-    load_sems, halo_sems, send_sem, recv_sems, last_sems,
+    signal, head, next_head, tail, outgoing, incoming, pieces, landed,
+    load_sems, halo_sems, send_sem, recv_sem, last_sems, wave_sem, ready_sems,
 ):
     f32, bf16 = jnp.float32, jnp.bfloat16
     band = lax.axis_index("band")
     s_me = lax.axis_index("stn")
     t_me = lax.axis_index("tm")
-    partners = [(ds, dt) for ds in (2, 3, 1, 0) for dt in range(T) if (ds, dt) != (0, 0)]
     rows_chunk = CHUNK * 64
     chunks = signal.shape[0] // rows_chunk
     halo_rows = DMAX // LANES
     tail_start = (chunks - 1) * rows_chunk
-
-    def partner(ds, dt):
-        return lax.rem(s_me + ds, S), lax.rem(t_me + dt, T)
 
     half = flat.shape[1] // 2
     loads = [
@@ -192,15 +187,49 @@
         load.start()
 
     barrier = pltpu.get_barrier_semaphore()
-    for ds, dt in partners:
-        s_to, t_to = partner(ds, dt)
-        pl.semaphore_signal(barrier, inc=1, device_id=(band, s_to, t_to), device_id_type=MESH)
+
+    def tell(sem, s_to, t_to):
+        pl.semaphore_signal(sem, inc=1, device_id=(band, s_to, t_to), device_id_type=MESH)
+
+    for dt in range(1, T):
+        tell(barrier, s_me, lax.rem(t_me + dt, T))
+
+    @pl.when(s_me > 0)
+    def _():
+        tell(barrier, s_me - 1, t_me)
+
+    @pl.when(s_me < S - 1)
+    def _():
+        tell(barrier, s_me + 1, t_me)
+
+    def greet(station):
+        pl.semaphore_wait(barrier, T - 1 + int(station > 0) + int(station < S - 1))
+        if station > 0:
+            pl.semaphore_wait(wave_sem, 1)
+        if station < S - 1:
+            tell(wave_sem, station + 1, t_me)
+        for lower in range(station):
+            tell(ready_sems.at[station], lower, t_me)
+
+    @pl.when(s_me == S - 1)
+    def _():
+        greet(S - 1)
 
     tail[pl.ds(rows_chunk + halo_rows, 8), :] = jnp.zeros((8, LANES), f32)
 
     @pl.when(t_me == T - 1)
     def _():
-        tail[pl.ds(rows_chunk, halo_rows), :] = jnp.zeros((halo_rows, LANES), f32)
+        next_head[...] = jnp.zeros_like(next_head)
+
+    def halo_copy():
+        return pltpu.make_async_remote_copy(
+            src_ref=head,
+            dst_ref=next_head,
+            send_sem=halo_sems.at[0],
+            recv_sem=halo_sems.at[1],
+            device_id=(band, s_me, lax.rem(t_me + T - 1, T)),
+            device_id_type=MESH,
+        )
 
     def lay_out(first_row, row_count):
         for row in range(first_row, first_row + row_count, 64):
@@ -211,6 +240,12 @@
 
     loads[0].wait()
     lay_out(0, 2 * rows_chunk)
+    head[...] = signal[pl.ds(0, halo_rows), :].astype(bf16)
+
+    @pl.when((s_me == S - 1) & (t_me > 0))
+    def _():
+        halo_copy().start()
+
     loads[1].wait()
     loads[2].wait()
     loads[3].wait()
@@ -270,33 +305,17 @@
             axis=1,
         ).astype(bf16)
 
-    def spectra_copy(group, ds, dt):
-        s_to, t_to = partner(ds, dt)
-        first_chunk, last_chunk = GROUPS[group]
-        part = pl.ds(first_chunk, last_chunk + 1 - first_chunk)
-        return pltpu.make_async_remote_copy(
+    def send(first_chunk, chunk_count, s_to, dt):
+        t_to = lax.rem(t_me + dt, T)
+        part = pl.ds(first_chunk, chunk_count)
+        pltpu.make_async_remote_copy(
             src_ref=outgoing.at[t_to * S + s_to, part],
             dst_ref=incoming.at[s_me * T + dt, part],
             send_sem=send_sem,
-            recv_sem=recv_sems.at[group],
+            recv_sem=recv_sem,
             device_id=(band, s_to, t_to),
             device_id_type=MESH,
-        )
-
-    def all_arrived(group):
-        first_chunk, last_chunk = GROUPS[group]
-        part = incoming.at[pl.ds(0, S * T - 1), pl.ds(first_chunk, last_chunk + 1 - first_chunk)]
-        pltpu.make_async_copy(part, part, recv_sems.at[group]).wait()
-
-    def halo_copy():
-        return pltpu.make_async_remote_copy(
-            src_ref=signal.at[pl.ds(0, halo_rows)],
-            dst_ref=tail.at[pl.ds(rows_chunk, halo_rows)],
-            send_sem=halo_sems.at[0],
-            recv_sem=halo_sems.at[1],
-            device_id=(band, s_me, lax.rem(t_me + T - 1, T)),
-            device_id_type=MESH,
-        )
+        ).start()
 
     for c in range(chunks):
         if c == 0:
@@ -313,26 +332,46 @@
             def _():
                 halo_copy().wait_recv()
 
+            tail[pl.ds(rows_chunk, halo_rows), :] = next_head[...].astype(f32)
+
         chunk_spectra(c)
         if c == 0:
-            pl.semaphore_wait(barrier, len(partners))
-
-            @pl.when(t_me > 0)
+            for station in range(S - 1):
+
+                @pl.when(s_me == station)
+                def _():
+                    greet(station)
+
+            @pl.when((s_me < S - 1) & (t_me > 0))
             def _():
                 halo_copy().start()
 
-        for group, (_, last_chunk) in enumerate(GROUPS):
-            if last_chunk == c:
-                for ds, dt in partners:
-                    spectra_copy(group, ds, dt).start()
+        for lower in range(S - 1):
+
+            @pl.when(lower < s_me)
+            def _():
+                for dt in range(T):
+                    send(c, 1, lower, dt)
+
+        for dt in range(1, T):
+            send(c, 1, s_me, dt)
         incoming[s_me * T, c] = outgoing[t_me * S + s_me, c]
+
+    for upper in range(1, S):
+
+        @pl.when(upper > s_me)
+        def _():
+            pl.semaphore_wait(ready_sems.at[upper], 1)
+            for dt in range(T):
+                send(0, chunks, upper, dt)
 
     pairs = [(i, j) for i in range(S) for j in range(i, S)]
     even = {pair: jnp.zeros((8, LANES), f32) for pair in pairs}
     odd = {pair: jnp.zeros((8, LANES), f32) for pair in pairs if pair[0] != pair[1]}
-    for group, (first_chunk, last_chunk) in enumerate(GROUPS):
-        all_arrived(group)
-        for dt, c in [(dt, c) for dt in range(T) for c in range(first_chunk, last_chunk + 1)]:
+    others = incoming.at[pl.ds(0, S * T - 1)]
+    pltpu.make_async_copy(others, others, recv_sem).wait()
+    for c in range(chunks):
+        for dt in range(T):
             tiles = [incoming[s * T + dt, c].astype(f32) for s in range(S)]
             for top in (0, 8):
                 part = [tile[top : top + 8] for tile in tiles]
@@ -412,6 +451,8 @@
         + [pltpu.VMEM(operand.shape, operand.dtype) for operand in operands[2:]]
         + [
             pltpu.VMEM((rows, LANES), jnp.float32),
+            pltpu.VMEM((DMAX // LANES, LANES), jnp.bfloat16),
+            pltpu.VMEM((DMAX // LANES, LANES), jnp.bfloat16),
             pltpu.VMEM((CHUNK * 64 + DMAX // LANES + 8, LANES), jnp.float32),
             pltpu.VMEM((blocks, chunks, 16, LANES), jnp.bfloat16),
             pltpu.VMEM((blocks, chunks, 16, LANES), jnp.bfloat16),
@@ -420,8 +461,10 @@
             pltpu.SemaphoreType.DMA((7,)),
             pltpu.SemaphoreType.DMA((2,)),
             pltpu.SemaphoreType.DMA,
-            pltpu.SemaphoreType.DMA((len(GROUPS),)),
+            pltpu.SemaphoreType.DMA,
             pltpu.SemaphoreType.DMA((2,)),
+            pltpu.SemaphoreType.REGULAR,
+            pltpu.SemaphoreType.REGULAR((stn_count,)),
         ],
         compiler_params=pltpu.CompilerParams(
             collective_id=0, has_side_effects=True, vmem_limit_bytes=60 << 20

time: 21.4 us -> 22.1 us (1.033)
  Pallas kernels: 19.2 us -> 19.8 us
    pallas_call x1, Pallas kernels: 19.2 us -> 19.8 us  [fused_on_device(): pl.pallas_call(functools.partial(fused_kernel, stn_count, tm_count, norm_...]
where the time goes in v3:
time: 22.1 us; the launch traced here: 21.9 us
  Pallas kernels  19.8 us (90%)
  local copies, waits for them, and re-layouts  1.39 us (6%)
  between operations  0.66 us (3%)
    pallas_call x1, Pallas kernels, fused_on_device(): pl.pallas_call(functools.partial(fused_kernel, stn_count, tm_count, norm_...  19.8 us
    reshape x1, local copies, waits for them, and re-layouts, fused_on_device(): return out.reshape(2, 1, stn_count, 1024)  1.39 us

profile of v3, /device:TPU:0, one launch (start us, length us, event | category | flops | bytes accessed | tf_op | source)
XLA Modules:
  0.0 21.9 jit_solution(575854346732297347)
XLA Ops:
  0.7 19.8 %correlate.1 = f32[8,1024]{1,0:T(8,128)} custom-call(bf16[1,131072]{1,0:T(2,128)(2,1)} %samples_hbm.1, s32[1,1]{1,0:T(1,128)S(6)} %copy.8.delays_hbm, s32[1,16]{1,0:T(1,128)} %fringe_hbm.1, bf16[128,128]{1,0:T(8,128)(2,1)} %constant.6.clone.first_hbm, f32[2,64,128]{2,1,0:T(8,128)} %constant.7.clone.twist_hbm, bf16[256,256]{1,0:T(8,128)(2,1)} %constant.8.clone.second_hbm), custom_call_target="tpu_custom_call" | custom-call | tf_op jit(solution)/shard_map/correlate/pallas_call | solution.py:442
  20.5 1.4 %reshape.3 = f32[2,1,4,1024]{3,2,0,1:T(4,128)} reshape(f32[8,1024]{1,0:T(8,128)} %correlate.1) | data formatting | bytes 65536 | tf_op jit(solution)/shard_map/reshape | solution.py:474

commit v4 on v2

--- a/solution.py
+++ b/solution.py
@@ -125,7 +125,7 @@
 
 LANES = 128
 CHUNK = 4
-GROUPS = ((0, 0), (1, 1), (2, 2), (3, 3))
+GROUPS = ((0, 2), (3, 3))
 
 
 def spectrum_tables(stn_count, tm_count):
@@ -157,21 +157,26 @@
     samples_hbm, delays_hbm, fringe_hbm, first_hbm, twist_hbm, second_hbm,
     out_ref,
     flat, delays_ref, fringe_ref, first_ref, twist_ref, second_ref,
-    signal, tail, outgoing, incoming, pieces, landed,
+    signal, head, next_head, tail, outgoing, incoming, pieces, landed,
     load_sems, halo_sems, send_sem, recv_sems, last_sems,
 ):
     f32, bf16 = jnp.float32, jnp.bfloat16
     band = lax.axis_index("band")
     s_me = lax.axis_index("stn")
     t_me = lax.axis_index("tm")
-    partners = [(ds, dt) for ds in (2, 3, 1, 0) for dt in range(T) if (ds, dt) != (0, 0)]
+    partners = [(ds, dt) for ds in (1, 2, 3, 0) for dt in range(T) if (ds, dt) != (0, 0)]
+    late = s_me == S - 1
     rows_chunk = CHUNK * 64
     chunks = signal.shape[0] // rows_chunk
     halo_rows = DMAX // LANES
     tail_start = (chunks - 1) * rows_chunk
 
     def partner(ds, dt):
-        return lax.rem(s_me + ds, S), lax.rem(t_me + dt, T)
+        if ds == 0:
+            return s_me, lax.rem(t_me + dt, T)
+        upward = ds - 1 + (s_me <= ds - 1).astype(jnp.int32)
+        downward = S - ds - (S - 1 - s_me <= ds - 1).astype(jnp.int32)
+        return lax.select(s_me >= S // 2, upward, downward), lax.rem(t_me + dt, T)
 
     half = flat.shape[1] // 2
     loads = [
@@ -200,7 +205,7 @@
 
     @pl.when(t_me == T - 1)
     def _():
-        tail[pl.ds(rows_chunk, halo_rows), :] = jnp.zeros((halo_rows, LANES), f32)
+        next_head[...] = jnp.zeros_like(next_head)
 
     def lay_out(first_row, row_count):
         for row in range(first_row, first_row + row_count, 64):
@@ -211,6 +216,7 @@
 
     loads[0].wait()
     lay_out(0, 2 * rows_chunk)
+    head[...] = signal[pl.ds(0, halo_rows), :].astype(bf16)
     loads[1].wait()
     loads[2].wait()
     loads[3].wait()
@@ -270,9 +276,8 @@
             axis=1,
         ).astype(bf16)
 
-    def spectra_copy(group, ds, dt):
+    def spectra_copy(group, first_chunk, last_chunk, ds, dt):
         s_to, t_to = partner(ds, dt)
-        first_chunk, last_chunk = GROUPS[group]
         part = pl.ds(first_chunk, last_chunk + 1 - first_chunk)
         return pltpu.make_async_remote_copy(
             src_ref=outgoing.at[t_to * S + s_to, part],
@@ -290,8 +295,8 @@
 
     def halo_copy():
         return pltpu.make_async_remote_copy(
-            src_ref=signal.at[pl.ds(0, halo_rows)],
-            dst_ref=tail.at[pl.ds(rows_chunk, halo_rows)],
+            src_ref=head,
+            dst_ref=next_head,
             send_sem=halo_sems.at[0],
             recv_sem=halo_sems.at[1],
             device_id=(band, s_me, lax.rem(t_me + T - 1, T)),
@@ -313,18 +318,36 @@
             def _():
                 halo_copy().wait_recv()
 
+            tail[pl.ds(rows_chunk, halo_rows), :] = next_head[...].astype(f32)
+
         chunk_spectra(c)
-        if c == 0:
+        def open_exchange():
             pl.semaphore_wait(barrier, len(partners))
 
             @pl.when(t_me > 0)
             def _():
                 halo_copy().start()
 
-        for group, (_, last_chunk) in enumerate(GROUPS):
+        if c == 0:
+            pl.when(late)(open_exchange)
+        if c == GROUPS[0][1]:
+            pl.when(jnp.logical_not(late))(open_exchange)
+
+        if c <= GROUPS[0][1]:
+
+            @pl.when(late)
+            def _():
+                for ds, dt in partners:
+                    spectra_copy(0, c, c, ds, dt).start()
+
+        for group, (first_chunk, last_chunk) in enumerate(GROUPS):
             if last_chunk == c:
-                for ds, dt in partners:
-                    spectra_copy(group, ds, dt).start()
+
+                @pl.when(jnp.logical_not(late) if group == 0 else True)
+                def _():
+                    for ds, dt in partners:
+                        spectra_copy(group, first_chunk, last_chunk, ds, dt).start()
+
         incoming[s_me * T, c] = outgoing[t_me * S + s_me, c]
 
     pairs = [(i, j) for i in range(S) for j in range(i, S)]
@@ -365,7 +388,7 @@
             put(j, S + i, -imag)
 
     def last_copy(ds):
-        s_to = lax.rem(s_me + ds, S)
+        s_to, _ = partner(ds, 0)
         return pltpu.make_async_remote_copy(
             src_ref=pieces.at[s_to],
             dst_ref=landed.at[s_me],
@@ -375,7 +398,7 @@
             device_id_type=MESH,
         )
 
-    for ds in (2, 3, 1):
+    for ds in (1, 2, 3):
         last_copy(ds).start()
     landed[s_me] = pieces[s_me]
     others = landed.at[pl.ds(0, S - 1)]
@@ -402,7 +425,7 @@
     operands = [samples, delays, fringe] + [jnp.asarray(table) for table in tables]
     out = pl.pallas_call(
         functools.partial(fused_kernel, stn_count, tm_count, norm_scale),
-        out_shape=jax.ShapeDtypeStruct((2 * stn_count, 1024), jnp.float32),
+        out_shape=pltpu.VMEM((2 * stn_count, 1024), jnp.float32),
         in_specs=[pl.BlockSpec(memory_space=pltpu.HBM)] * len(operands),
         out_specs=pl.BlockSpec(memory_space=pltpu.VMEM),
         scratch_shapes=[
@@ -412,6 +435,8 @@
         + [pltpu.VMEM(operand.shape, operand.dtype) for operand in operands[2:]]
         + [
             pltpu.VMEM((rows, LANES), jnp.float32),
+            pltpu.VMEM((DMAX // LANES, LANES), jnp.bfloat16),
+            pltpu.VMEM((DMAX // LANES, LANES), jnp.bfloat16),
             pltpu.VMEM((CHUNK * 64 + DMAX // LANES + 8, LANES), jnp.float32),
             pltpu.VMEM((blocks, chunks, 16, LANES), jnp.bfloat16),
             pltpu.VMEM((blocks, chunks, 16, LANES), jnp.bfloat16),

time: 21.4 us -> 18.7 us (0.87)
  Pallas kernels: 19.2 us -> 17.3 us
  local copies, waits for them, and re-layouts: 1.39 us -> 0.63 us
    pallas_call x1, Pallas kernels: 19.2 us -> 17.3 us  [fused_on_device(): pl.pallas_call(functools.partial(fused_kernel, stn_count, tm_count, norm_...]
    reshape x1, local copies, waits for them, and re-layouts: 1.39 us -> 0.63 us  [fused_on_device(): return out.reshape(2, 1, stn_count, 1024)]
where the time goes in v4:
time: 18.7 us; the launch traced here: 18.6 us
  Pallas kernels  17.3 us (93%)
  between operations  0.66 us (4%)
  local copies, waits for them, and re-layouts  0.63 us (3%)
    pallas_call x1, Pallas kernels, fused_on_device(): pl.pallas_call(functools.partial(fused_kernel, stn_count, tm_count, norm_...  17.3 us
    reshape x1, local copies, waits for them, and re-layouts, fused_on_device(): return out.reshape(2, 1, stn_count, 1024)  0.63 us

profile of v4, /device:TPU:0, one launch (start us, length us, event | category | flops | bytes accessed | tf_op | source)
XLA Modules:
  0.0 18.6 jit_solution(7313354144553051578)
XLA Ops:
  0.7 17.3 %correlate.1 = f32[8,1024]{1,0:T(8,128)S(1)} custom-call(bf16[1,131072]{1,0:T(2,128)(2,1)} %samples_hbm.1, s32[1,1]{1,0:T(1,128)S(6)} %copy.8.delays_hbm, s32[1,16]{1,0:T(1,128)} %fringe_hbm.1, bf16[128,128]{1,0:T(8,128)(2,1)} %constant.6.clone.first_hbm, f32[2,64,128]{2,1,0:T(8,128)} %constant.7.clone.twist_hbm, bf16[256,256]{1,0:T(8,128)(2,1)} %constant.8.clone.second_hbm), custom_call_target="tpu_custom_call" | custom-call | tf_op jit(solution)/shard_map/correlate/pallas_call | solution.py:426
  17.9 0.6 %reshape.3 = f32[2,1,4,1024]{3,2,0,1:T(4,128)} reshape(f32[8,1024]{1,0:T(8,128)S(1)} %correlate.1) | data formatting | bytes 65536 | tf_op jit(solution)/shard_map/reshape | solution.py:456

commit v5 on v4

--- a/solution.py
+++ b/solution.py
@@ -164,7 +164,7 @@
     band = lax.axis_index("band")
     s_me = lax.axis_index("stn")
     t_me = lax.axis_index("tm")
-    partners = [(ds, dt) for ds in (1, 2, 3, 0) for dt in range(T) if (ds, dt) != (0, 0)]
+    partners = [(ds, dt) for ds in (1, 2, 3, 0) for dt in (2, 3, 0, 1) if (ds, dt) != (0, 0)]
     late = s_me == S - 1
     rows_chunk = CHUNK * 64
     chunks = signal.shape[0] // rows_chunk
@@ -404,7 +404,8 @@
     others = landed.at[pl.ds(0, S - 1)]
     pltpu.make_async_copy(others, others, last_sems.at[1]).wait()
     for s in range(S):
-        out_ref[:, pl.ds(s * 2 * LANES, 2 * LANES)] = landed[s]
+        for part in range(2):
+            out_ref[part, :, pl.ds(s * 2 * LANES, 2 * LANES)] = landed[s, S * part : S * part + S]
 
     pltpu.make_async_copy(others, others, last_sems.at[0]).wait()
     sent = outgoing.at[pl.ds(0, S * T - 1)]
@@ -425,7 +426,7 @@
     operands = [samples, delays, fringe] + [jnp.asarray(table) for table in tables]
     out = pl.pallas_call(
         functools.partial(fused_kernel, stn_count, tm_count, norm_scale),
-        out_shape=pltpu.VMEM((2 * stn_count, 1024), jnp.float32),
+        out_shape=pltpu.VMEM((2, stn_count, 1024), jnp.float32),
         in_specs=[pl.BlockSpec(memory_space=pltpu.HBM)] * len(operands),
         out_specs=pl.BlockSpec(memory_space=pltpu.VMEM),
         scratch_shapes=[
@@ -453,7 +454,7 @@
         ),
         name="correlate",
     )(*operands)
-    return out.reshape(2, 1, stn_count, 1024)
+    return out[:, None]
 
 
 def solution(mesh):

time: 18.7 us -> 18.7 us (level)
    reshape x1 -> x0, local copies, waits for them, and re-layouts: 0.63 us -> none  [fused_on_device(): return out.reshape(2, 1, stn_count, 1024)]
    unnamed x0 -> x1, local copies, waits for them, and re-layouts: none -> 0.62 us
where the time goes in v5:
time: 18.7 us; the launch traced here: 18.5 us
  Pallas kernels  17.3 us (93%)
  between operations  0.66 us (4%)
  local copies, waits for them, and re-layouts  0.62 us (3%)
    pallas_call x1, Pallas kernels, fused_on_device(): pl.pallas_call(functools.partial(fused_kernel, stn_count, tm_count, norm_...  17.3 us
    unnamed x1, local copies, waits for them, and re-layouts  0.62 us

profile of v5, /device:TPU:0, one launch (start us, length us, event | category | flops | bytes accessed | tf_op | source)
XLA Modules:
  0.0 18.5 jit_solution(13958939873234617046)
XLA Ops:
  0.7 17.3 %correlate.1 = f32[2,4,1024]{2,1,0:T(4,128)S(1)} custom-call(bf16[1,131072]{1,0:T(2,128)(2,1)} %samples_hbm.1, s32[1,1]{1,0:T(1,128)S(6)} %copy.10.delays_hbm, s32[1,16]{1,0:T(1,128)} %fringe_hbm.1, bf16[128,128]{1,0:T(8,128)(2,1)} %constant.6.clone.first_hbm, f32[2,64,128]{2,1,0:T(8,128)} %constant.7.clone.twist_hbm, bf16[256,256]{1,0:T(8,128)(2,1)} %constant.8.clone.second_hbm), custom_call_target="tpu_custom_call" | custom-call | tf_op jit(solution)/shard_map/correlate/pallas_call | solution.py:427
  17.9 0.6 %copy.9 = f32[2,1,4,1024]{3,2,1,0:T(4,128)} copy(f32[2,1,4,1024]{3,2,1,0:T(4,128)S(1)} %bitcast.3) | data formatting | bytes 65536

commit v6 on v5

--- a/solution.py
+++ b/solution.py
@@ -165,7 +165,7 @@
     s_me = lax.axis_index("stn")
     t_me = lax.axis_index("tm")
     partners = [(ds, dt) for ds in (1, 2, 3, 0) for dt in (2, 3, 0, 1) if (ds, dt) != (0, 0)]
-    late = s_me == S - 1
+    late = s_me >= S // 2
     rows_chunk = CHUNK * 64
     chunks = signal.shape[0] // rows_chunk
     halo_rows = DMAX // LANES
@@ -333,12 +333,12 @@
         if c == GROUPS[0][1]:
             pl.when(jnp.logical_not(late))(open_exchange)
 
-        if c <= GROUPS[0][1]:
+        if c in (0, GROUPS[0][1]):
 
             @pl.when(late)
             def _():
                 for ds, dt in partners:
-                    spectra_copy(0, c, c, ds, dt).start()
+                    spectra_copy(0, min(c, 1), c, ds, dt).start()
 
         for group, (first_chunk, last_chunk) in enumerate(GROUPS):
             if last_chunk == c:

time: 18.7 us -> 18.6 us (level)
  no operation moved by 1% of the time
where the time goes in v6:
time: 18.6 us; the launch traced here: 18.5 us
  Pallas kernels  17.2 us (92%)
  between operations  0.66 us (4%)
  local copies, waits for them, and re-layouts  0.62 us (3%)
    pallas_call x1, Pallas kernels, fused_on_device(): pl.pallas_call(functools.partial(fused_kernel, stn_count, tm_count, norm_...  17.2 us
    unnamed x1, local copies, waits for them, and re-layouts  0.62 us

profile of v6, /device:TPU:0, one launch (start us, length us, event | category | flops | bytes accessed | tf_op | source)
XLA Modules:
  0.0 18.5 jit_solution(840810977644866090)
XLA Ops:
  0.7 17.2 %correlate.1 = f32[2,4,1024]{2,1,0:T(4,128)S(1)} custom-call(bf16[1,131072]{1,0:T(2,128)(2,1)} %samples_hbm.1, s32[1,1]{1,0:T(1,128)S(6)} %copy.10.delays_hbm, s32[1,16]{1,0:T(1,128)} %fringe_hbm.1, bf16[128,128]{1,0:T(8,128)(2,1)} %constant.6.clone.first_hbm, f32[2,64,128]{2,1,0:T(8,128)} %constant.7.clone.twist_hbm, bf16[256,256]{1,0:T(8,128)(2,1)} %constant.8.clone.second_hbm), custom_call_target="tpu_custom_call" | custom-call | tf_op jit(solution)/shard_map/correlate/pallas_call | solution.py:427
  17.9 0.6 %copy.9 = f32[2,1,4,1024]{3,2,1,0:T(4,128)} copy(f32[2,1,4,1024]{3,2,1,0:T(4,128)S(1)} %bitcast.3) | data formatting | bytes 65536
